TPU v7x, 32 devices: a whole 2x2x4 slice. The times are simulated.
32 devices in a mesh: groups: 2 (over y), mp: 4 (over z), layer: 2 (over x), pool: 2 (over core).
Axes of the slice: x: 2, y: 2, z: 4, core: 2. Of those that a mesh axis runs over, the one named last changes fastest.
Arguments:
- enc_rows: float32 [2048, 4096], P(('groups', 'mp', 'layer', 'pool')), parts along dimension 0, may hold values from -6 to 6
- kv_weight: bfloat16 [2, 4096, 2, 4096], P('layer', 'pool', None, 'mp'), may hold values from -0.09375 to 0.09375
- lengths: int32 [32], P('groups'), parts along dimension 0, may hold values from 1 to 128, 1024 in all
- slot_of: int32 [32], P('groups'), parts along dimension 0, may hold values from 0 to 15, each once
- order: int32 [32], P('groups'), parts along dimension 0, may hold values from 0 to 15, each once
Outputs:
- kv_cache: bfloat16 [2, 32, 128, 2, 4096], P('layer', ('groups', 'pool'), None, None, 'mp'), parts along dimension 1
There are 2 independent parts, one for each index of `groups`. A program takes and returns all parts, laid end to end along the dimension named above; an argument that names none is the same for every part. Nothing has to cross between parts.
Inputs may be any that keep to these rules, and one draw needn't show every extreme that they name: The 16 lengths add up to exactly 1024, and some request has exactly 128 rows. `slot_of`: a permutation of the 16 slots. A permutation of the 16 requests; their rows lie in enc_rows one request after another in this order.
All inputs are finite; a program needn't handle non-finite values.
Results may differ from a plain program's by a relative error of at most 0.0049.
Values may be sent and summed in bfloat16 or wider, within the bound.
A program may use at most 128 MiB of HBM per device.

v0:
```python
import jax
import jax.numpy as jnp
from jax import lax
from jax.sharding import PartitionSpec as P

MAXLEN = 128


def pack_tables(lengths, slot_of, order):
    count_all = lengths.shape[0]
    request_ids = lax.iota(jnp.int32, count_all)
    selector = (order[:, None] == request_ids[None, :]).astype(jnp.int32)
    order_length = jnp.sum(selector * lengths[None, :], axis=1)
    order_begin = jnp.cumsum(order_length) - order_length
    begins = jnp.sum(selector * order_begin[:, None], axis=0)
    owner = (slot_of[:, None] == request_ids[None, :]).astype(jnp.int32)
    request = jnp.sum(owner * request_ids[:, None], axis=0)
    chooser = (request[:, None] == request_ids[None, :]).astype(jnp.int32)
    slot_begin = jnp.sum(chooser * begins[None, :], axis=1)
    slot_size = jnp.sum(chooser * lengths[None, :], axis=1)
    return (slot_begin, slot_size)


def place_rows(values, positions, slot_begin, slot_size):
    slot_count = slot_begin.shape[0]
    slot_index = positions // MAXLEN
    offset = positions % MAXLEN
    selector = (slot_index[:, None] == lax.iota(jnp.int32, slot_count)[None, :]).astype(jnp.int32)
    first_row = jnp.sum(selector * slot_begin[None, :], axis=1)
    row_limit = jnp.sum(selector * slot_size[None, :], axis=1)
    inside = offset < row_limit
    source = jnp.where(inside, first_row + offset, 0)
    taken = jnp.take(values, source, axis=0)
    return jnp.where(inside[:, None], taken, jnp.zeros((), values.dtype))


def per_device(enc_rows, kv_weight, lengths, slot_of, order):
    slot_begin, slot_size = pack_tables(lengths, slot_of, order)
    slot_count = lengths.shape[0]
    half_slots = slot_count // lax.axis_size("pool")
    head_width = kv_weight.shape[3]
    row_block = enc_rows.astype(jnp.bfloat16)
    weight = lax.all_gather(kv_weight[0], "pool", axis=0, tiled=True)
    flat_weight = weight.reshape(weight.shape[0], 2 * head_width)
    key_value = jnp.dot(
        lax.all_gather(row_block, ("mp", "layer", "pool"), axis=0, tiled=True),
        flat_weight,
        preferred_element_type=jnp.float32,
    ).astype(jnp.bfloat16)
    own_slots = lax.axis_index("pool") * (half_slots * MAXLEN) + lax.iota(
        jnp.int32, half_slots * MAXLEN
    )
    placed = place_rows(key_value, own_slots, slot_begin, slot_size)
    return placed.reshape(1, half_slots, MAXLEN, 2, head_width)


def solution(mesh):
    return jax.shard_map(
        per_device,
        mesh=mesh,
        in_specs=(
            P(("groups", "mp", "layer", "pool"), None),
            P("layer", "pool", None, "mp"),
            P("groups"),
            P("groups"),
            P("groups"),
        ),
        out_specs=P("layer", ("groups", "pool"), None, None, "mp"),
        check_vma=False,
    )
```

profile of v0, /device:TPU:0, one launch (start us, length us, event | category | flops | bytes accessed | tf_op | source)
XLA Modules:
  0.0 177.6 jit_solution(12563116005991668408)
XLA Ops:
  6.5 0.0 all-gather.6.cloned.1.call-start
  6.5 0.0 copy-start
  6.5 0.0 copy-start.1
  6.5 0.0 copy-start.3
  6.5 0.0 copy-start.2
  6.5 0.7 all-gather.6.cloned.1.call-update
  7.3 0.0 all-gather.4.cloned.1.call-start
  7.3 0.5 copy-done
  7.8 0.8 convert_element_type.4
  8.6 0.0 all-gather.4.cloned.1.call-update
  8.6 0.0 copy-done.1
  8.6 0.0 copy-done.3
  8.7 0.2 select_reduce_fusion.4
  8.8 0.1 copy.10
  9.0 0.1 reduce
  9.1 0.0 copy-done.2
  9.1 0.1 select_reduce_fusion.3
  9.2 0.2 select_reduce_fusion.2
  9.4 0.1 select_reduce_fusion
  9.6 32.1 %all-gather.6.cloned.1.call-done = bf16[1,4096,2,1024]{3,2,0,1:T(2,128)(2,1)} async-done(((bf16[1,2048,2,1024]{3,2,0,1:T(2,128)(2,1)}), bf16[1,4096,2,1024]{3,2,0,1:T(2,128)(2,1)}) %all-gather.6.cloned.1.call-update) | async-done | bytes 16777232 | tf_op jit(solution)/shard_map/all_gather | solution.py:43
  41.7 17.1 %copy.12 = bf16[512,8,2,1024]{3,1,2,0:T(8,128)(2,1)} copy(bf16[512,8,2,1024]{3,2,1,0:T(2,128)(2,1)} %bitcast.22) | data formatting | bytes 33554432
  58.8 61.1 %all-gather.4.cloned.1.call-done = bf16[1024,4096]{1,0:T(8,128)(2,1)} async-done(((bf16[64,4096]{1,0:T(8,128)(2,1)}), bf16[1024,4096]{1,0:T(8,128)(2,1)}) %all-gather.4.cloned.1.call-update) | async-done | bytes 8388624 | tf_op jit(solution)/shard_map/all_gather | solution.py:46
  120.0 23.6 %convolution_convert_fusion = bf16[1024,2048]{1,0:T(8,128)(2,1)} fusion(bf16[1024,4096]{1,0:T(8,128)(2,1)} %all-gather.4.cloned.1.call-done, bf16[4096,2048]{1,0:T(8,128)(2,1)} %bitcast.23), kind=kOutput, calls=%fused_computation.3 | convolution fusion | flops 17181966336 | bytes 29360128 | tf_op jit(solution)/shard_map/dot_general | solution.py:45
  143.6 11.6 %gather_fusion = bf16[1024,2048]{1,0:T(8,128)(2,1)} fusion(bf16[1024,2048]{1,0:T(8,128)(2,1)} %convolution_convert_fusion, s32[1024]{0:T(1024)S(1)} %broadcast_clamp_fusion), kind=kCustom, calls=%fused_computation | custom fusion | bytes 8392704 | tf_op jit(solution)/shard_map/jit(_take)/gather | solution.py:33
  155.1 7.8 %gather.7 = bf16[1,8,128,2,1024]{4,3,2,1,0:T(2,128)(2,1)} reshape(bf16[1024,2048]{1,0:T(8,128)(2,1)} %gather_fusion) | data formatting | bytes 8388608 | tf_op jit(solution)/shard_map/jit(_take)/gather | solution.py:33
  162.9 7.8 %broadcast_select_fusion.1 = bf16[1,8,128,2,1024]{4,3,2,1,0:T(2,128)(2,1)} fusion(pred[8,128]{1,0:T(8,128)(4,1)S(1)} %get-tuple-element.10, bf16[1,8,128,2,1024]{4,3,2,1,0:T(2,128)(2,1)} %gather.7, pred[8,128]{1,0:T(8,128)(4,1)S(1)} %get-tuple-element.9), kind=kLoop, calls=%fused_computation.2 | loop fusion | flops 4194304 | bytes 8390656 | tf_op jit(solution)/shard_map/jit(_where)/select_n | solution.py:34
  (6 shorter events, 0.1 us)
Async XLA Ops:
  6.5 35.2 %all-gather.6.cloned.1.call-start = ((), (), s32[]{:S(2)}) async-start(), calls=%async_computation.1 | async-start | bytes 25165824 | tf_op jit(solution)/shard_map/all_gather | solution.py:43
  6.5 1.2 copy-start
  6.5 2.1 %copy-start.1 = (s32[16]{0:T(128)S(1)}, s32[16]{0:T(128)}, u32[]{:S(2)}) copy-start(s32[16]{0:T(128)} %param.9) | copy-start | bytes 196
  6.5 2.1 %copy-start.3 = (s32[16]{0:T(128)S(1)}, s32[16]{0:T(128)}, u32[]{:S(2)}) copy-start(s32[16]{0:T(128)} %param.7) | copy-start | bytes 196
  6.5 2.6 %copy-start.2 = (s32[16]{0:T(128)S(1)}, s32[16]{0:T(128)}, u32[]{:S(2)}) copy-start(s32[16]{0:T(128)} %param.8) | copy-start | bytes 196
  7.3 112.7 %all-gather.4.cloned.1.call-start = ((), (), s32[]{:S(2)}) async-start(), calls=%async_computation | async-start | bytes 8912896 | tf_op jit(solution)/shard_map/all_gather | solution.py:46
Sparse Core Ops, SparseCore 0:
  8.9 32.7 all-gather.5
  43.9 76.0 all-gather.3
where the time goes:
time: 178 us
  waiting for transfers between devices  94 us (53%)
  local copies, waits for them, and re-layouts  37 us (21%)
  matrix products  23.6 us (13%)
  between operations  13.5 us (8%)
  other arithmetic  9.47 us (5%)
    all_gather x1, waiting for transfers between devices, per_device(): lax.all_gather(row_block, ('mp', 'layer', 'pool'), axis=0, tiled=True)  61.1 us
    all_gather x1, waiting for transfers between devices, per_device(): weight = lax.all_gather(kv_weight[0], 'pool', axis=0, tiled=True)  32.1 us
    dot_general x1, matrix products, per_device(): jnp.dot(lax.all_gather(row_block, ('mp', 'layer', 'pool'), axis=0, tiled=...  23.6 us
    gather x2, local copies, waits for them, and re-layouts, place_rows(): taken = jnp.take(values, source, axis=0)  19.3 us
    unnamed x9, local copies, waits for them, and re-layouts  17.6 us
    select_n x1, other arithmetic, place_rows(): return jnp.where(inside[:, None], taken, jnp.zeros((), values.dtype))  7.85 us
  transfers between devices with their start and end apart: 2, of which 2 were waited for; matrix products, arithmetic and copies ran while one was open for 11% of the time, Pallas kernels for 0%

commit v1 on v0

--- a/solution.py
+++ b/solution.py
@@ -1,8 +1,11 @@
+import functools
+
 import jax
 import jax.numpy as jnp
 from jax import lax
+from jax.experimental import pallas as pl
+from jax.experimental.pallas import tpu as pltpu
 from jax.sharding import PartitionSpec as P
-
 MAXLEN = 128
 
 
@@ -34,11 +37,261 @@
     return jnp.where(inside[:, None], taken, jnp.zeros((), values.dtype))
 
 
+def gather_multiply(mp_size, x_ref, w_hbm, kv_ref, w_raw, w_flat, x_send, rows, acc, part, other, *sems):
+    w_sem, x_ss, x_rs, r_ss, r_rs, l_ss, l_rs, p_ss, p_rs = sems
+    mesh_id = pl.DeviceIdType.MESH
+    ring = 2 * mp_size
+    count, half = x_send.shape
+    width = w_flat.shape[1]
+    pool = lax.axis_index("pool")
+    layer = lax.axis_index("layer")
+    mp = lax.axis_index("mp")
+    here = mp + layer * (ring - 1 - 2 * mp)
+
+    def place(steps):
+        at = (here + steps + ring) % ring
+        on_layer = at // mp_size
+        return at + on_layer * (ring - 1 - 2 * at), on_layer
+
+    def chip(steps):
+        on_mp, on_layer = place(steps)
+        return on_mp * 2 + on_layer
+
+    def device(steps):
+        on_mp, on_layer = place(steps)
+        return {"mp": on_mp, "layer": on_layer}
+
+    partner = {"pool": 1 - pool}
+    depth = half // 4
+
+    def weight_copy(i):
+        return pltpu.make_async_copy(
+            w_hbm.at[pl.ds(i * depth, depth)], w_raw.at[pl.ds(i * depth, depth)], w_sem.at[i]
+        )
+
+    for i in range(4):
+        weight_copy(i).start()
+    barrier = pltpu.get_barrier_semaphore()
+    for target in (device(1), device(-1), partner):
+        pl.semaphore_signal(barrier, inc=1, device_id=target, device_id_type=mesh_id)
+    mine = chip(0)
+    rows[mine, pool] = x_ref[:, pl.ds(pl.multiple_of(pool * half, half), half)].astype(jnp.bfloat16)
+    x_send[...] = x_ref[:, pl.ds(pl.multiple_of((1 - pool) * half, half), half)].astype(jnp.bfloat16)
+    pl.semaphore_wait(barrier, 3)
+
+    def send(k, direction):
+        last = k == ring - 2
+        second = (k % 2 == 1) or (last and direction < 0)
+        core = 1 - pool if second else pool
+        slot = rows.at[chip(-direction * (k // 2)), core]
+        ss, rs = (r_ss, r_rs) if direction > 0 else (l_ss, l_rs)
+        return pltpu.make_async_remote_copy(
+            src_ref=slot, dst_ref=slot, send_sem=ss.at[k], recv_sem=rs.at[k],
+            device_id=device(direction), device_id_type=mesh_id,
+        )
+
+    def swap_rows():
+        return pltpu.make_async_remote_copy(
+            src_ref=x_send, dst_ref=rows.at[mine, pool], send_sem=x_ss, recv_sem=x_rs,
+            device_id=partner, device_id_type=mesh_id,
+        )
+
+    def arrived(k, direction):
+        last = k == ring - 2
+        second = (k % 2 == 1) or (last and direction < 0)
+        core = 1 - pool if second else pool
+        slot = rows.at[chip(-direction * (k // 2 + 1)), core]
+        ss, rs = (r_ss, r_rs) if direction > 0 else (l_ss, l_rs)
+        pltpu.make_async_remote_copy(
+            src_ref=slot, dst_ref=slot, send_sem=ss.at[k], recv_sem=rs.at[k],
+            device_id=device(direction), device_id_type=mesh_id,
+        ).wait_recv()
+
+    def flatten(i):
+        weight_copy(i).wait()
+        piece = 32
+
+        @pl.loop(0, depth // piece)
+        def _(t):
+            start = pl.multiple_of(i * depth + t * piece, piece)
+            w_flat[pl.ds(start, piece), :] = w_raw[pl.ds(start, piece)].reshape(piece, width)
+
+    def swap_part(m, at):
+        return pltpu.make_async_remote_copy(
+            src_ref=part.at[at], dst_ref=other.at[at], send_sem=p_ss.at[m], recv_sem=p_rs.at[m],
+            device_id=partner, device_id_type=mesh_id,
+        )
+
+    def multiply(chips, m):
+        columns = 256
+
+        @pl.loop(0, width // columns)
+        def _(t):
+            span = pl.ds(pl.multiple_of(t * columns, columns), columns)
+            left = jnp.concatenate([rows[c].reshape(2 * count, half) for c in chips], axis=0)
+            product = jnp.dot(left, w_flat[:, span], preferred_element_type=jnp.float32)
+            for i, c in enumerate(chips):
+                one = product[i * 2 * count : (i + 1) * 2 * count]
+                acc[c, :, span] = one
+                part[c, :, span] = one.astype(jnp.bfloat16)
+
+        for i, c in enumerate(chips):
+            swap_part(m + i, c).start()
+
+    def finish(chips, m):
+        for i, c in enumerate(chips):
+            swap_part(m + i, c).wait_recv()
+
+            @pl.loop(0, 2 * count // 16)
+            def _(t):
+                span = pl.ds(pl.multiple_of(t * 16, 16), 16)
+                total = acc[c, span, :] + other[c, span, :].astype(jnp.float32)
+                kv_ref[c, span, :] = total.astype(jnp.bfloat16)
+
+    send(0, 1).start()
+    send(0, -1).start()
+    swap_rows().start()
+    swap_rows().wait_recv()
+    send(1, 1).start()
+    send(1, -1).start()
+    flatten(0)
+    flatten(1)
+    reach = ring // 2
+    waiting = None
+    for k in range(ring - 1):
+        if k == ring - 2:
+            finish(*waiting)
+        arrived(k, 1)
+        arrived(k, -1)
+        ahead = k + 2
+        if ahead < ring - 2:
+            send(ahead, 1).start()
+            send(ahead, -1).start()
+        elif ahead == ring - 2:
+            send(ahead, 1).start()
+        elif ahead == ring - 1:
+            send(ring - 2, -1).start()
+        if k == 0:
+            flatten(2)
+            flatten(3)
+            multiply([mine], 0)
+            waiting = ([mine], 0)
+        elif k % 2 == 1:
+            d = (k + 1) // 2
+            chips = [chip(-d), chip(d)]
+            multiply(chips, 2 * d - 1)
+            finish(*waiting)
+            waiting = (chips, 2 * d - 1)
+    multiply([chip(reach)], ring - 1)
+    finish([chip(reach)], ring - 1)
+    swap_rows().wait_send()
+    for k in range(ring - 1):
+        send(k, 1).wait_send()
+        send(k, -1).wait_send()
+    swap_part(0, mine).wait_send()
+    for d in range(1, reach):
+        swap_part(2 * d - 1, chip(-d)).wait_send()
+        swap_part(2 * d, chip(d)).wait_send()
+    swap_part(ring - 1, chip(reach)).wait_send()
+
+
+def key_values(enc_rows, weight, mp_size):
+    count, features = enc_rows.shape
+    half, _, head_width = weight.shape
+    width, ring = 2 * head_width, 2 * mp_size
+    dma = pltpu.SemaphoreType.DMA
+    block = (ring, 2 * count, width)
+    packed = pl.pallas_call(
+        functools.partial(gather_multiply, mp_size),
+        out_shape=jax.ShapeDtypeStruct(block, jnp.bfloat16),
+        in_specs=[pl.BlockSpec(memory_space=pltpu.VMEM), pl.BlockSpec(memory_space=pl.ANY)],
+        out_specs=pl.BlockSpec(memory_space=pltpu.VMEM),
+        scratch_shapes=[
+            pltpu.VMEM(weight.shape, jnp.bfloat16),
+            pltpu.VMEM((half, width), jnp.bfloat16),
+            pltpu.VMEM((count, half), jnp.bfloat16),
+            pltpu.VMEM((ring, 2, count, half), jnp.bfloat16),
+            pltpu.VMEM(block, jnp.float32),
+            pltpu.VMEM(block, jnp.bfloat16),
+            pltpu.VMEM(block, jnp.bfloat16),
+            dma((4,)),
+            dma,
+            dma,
+            dma((ring - 1,)),
+            dma((ring - 1,)),
+            dma((ring - 1,)),
+            dma((ring - 1,)),
+            dma((ring,)),
+            dma((ring,)),
+        ],
+        compiler_params=pltpu.CompilerParams(
+            collective_id=0, has_side_effects=True, vmem_limit_bytes=56 << 20
+        ),
+        name="gather_multiply",
+    )(enc_rows, weight)
+    return packed.reshape(ring * 2 * count, width)
+
+
+def place_kernel(window, lengths, slot_of, order, kv_ref, out_ref, begins, request):
+    slot_count = lengths.shape[0]
+    step = pl.program_id(0)
+
+    @pl.when(step == 0)
+    def _():
+        def one(i, begin):
+            begins[order[i]] = begin
+            request[slot_of[i]] = i
+            return begin + lengths[order[i]]
+
+        lax.fori_loop(0, slot_count, one, jnp.int32(0))
+
+    who = request[lax.axis_index("pool") * pl.num_programs(0) + step]
+    size, begin = lengths[who], begins[who]
+    base = pl.multiple_of(jnp.minimum((begin // 16) * 16, kv_ref.shape[0] - window), 16)
+    shape = (MAXLEN, window)
+    position = lax.broadcasted_iota(jnp.int32, shape, 0)
+    source = lax.broadcasted_iota(jnp.int32, shape, 1)
+    chosen = (source == position + (begin - base)) & (position < size)
+    picked = jnp.where(chosen, 1.0, 0.0).astype(jnp.bfloat16)
+    taken = jnp.dot(picked, kv_ref[pl.ds(base, window), :], preferred_element_type=jnp.float32)
+    out_ref[0, 0] = taken.astype(jnp.bfloat16).reshape(out_ref.shape[2:])
+
+
+def place_slots(key_value, lengths, slot_of, order, half_slots):
+    width = key_value.shape[1]
+    slot_count = lengths.shape[0]
+    smem = pl.BlockSpec(memory_space=pltpu.SMEM)
+    shape = (1, half_slots, MAXLEN, 2, width // 2)
+    return pl.pallas_call(
+        functools.partial(place_kernel, 2 * MAXLEN),
+        grid=(half_slots,),
+        out_shape=jax.ShapeDtypeStruct(shape, jnp.bfloat16),
+        in_specs=[smem, smem, smem, pl.BlockSpec(memory_space=pltpu.VMEM)],
+        out_specs=pl.BlockSpec((1, 1, MAXLEN, 2, width // 2), lambda s: (0, s, 0, 0, 0)),
+        scratch_shapes=[
+            pltpu.SMEM((slot_count,), jnp.int32),
+            pltpu.SMEM((slot_count,), jnp.int32),
+        ],
+        compiler_params=pltpu.CompilerParams(vmem_limit_bytes=32 << 20),
+        name="place_slots",
+    )(lengths, slot_of, order, key_value)
+
+
 def per_device(enc_rows, kv_weight, lengths, slot_of, order):
+    half_slots = lengths.shape[0] // lax.axis_size("pool")
+    head_width = kv_weight.shape[3]
+    mp_size = lax.axis_size("mp")
+    ring_fits = (
+        lax.axis_size("layer") == 2
+        and lax.axis_size("pool") == 2
+        and 2 <= mp_size <= 8
+        and enc_rows.shape[0] % 16 == 0
+        and head_width % 128 == 0
+    )
+    if ring_fits:
+        key_value = key_values(enc_rows, kv_weight[0], mp_size)
+        return place_slots(key_value, lengths, slot_of, order, half_slots)
     slot_begin, slot_size = pack_tables(lengths, slot_of, order)
-    slot_count = lengths.shape[0]
-    half_slots = slot_count // lax.axis_size("pool")
-    head_width = kv_weight.shape[3]
     row_block = enc_rows.astype(jnp.bfloat16)
     weight = lax.all_gather(kv_weight[0], "pool", axis=0, tiled=True)
     flat_weight = weight.reshape(weight.shape[0], 2 * head_width)

time: 178 us -> 62.5 us (0.35)
  waiting for transfers between devices: 94 us -> 0 us
  Pallas kernels: 0 us -> 60.1 us
  local copies, waits for them, and re-layouts: 37 us -> 2.19 us
  matrix products: 23.6 us -> 0 us
  between operations: 13.5 us -> 0.04 us
  other arithmetic: 9.47 us -> 0 us
    all_gather x2 -> x0, waiting for transfers between devices: 93.3 us -> none  [the longest x1 61.1 us: per_device(): lax.all_gather(row_block, ('mp', 'layer', 'pool'), axis=0, tiled=True)]
    pallas_call x0 -> x2, Pallas kernels: none -> 60.1 us  [the longest x1 54.3 us: key_values(): pl.pallas_call(functools.partial(gather_multiply, mp_size), out_shape=jax...]
    dot_general x1 -> x0, matrix products: 23.6 us -> none  [per_device(): jnp.dot(lax.all_gather(row_block, ('mp', 'layer', 'pool'), axis=0, tiled=...]
    gather x2 -> x0, local copies, waits for them, and re-layouts: 19.3 us -> none  [place_rows(): taken = jnp.take(values, source, axis=0)]
    unnamed x9 -> x8, local copies, waits for them, and re-layouts: 17.6 us -> 2.19 us
    select_n x3 -> x0, other arithmetic: 7.89 us -> none  [the longest x1 7.85 us: place_rows(): return jnp.where(inside[:, None], taken, jnp.zeros((), values.dtype))]
  transfers between devices with their start and end apart: 2 -> 0, of which waited for: 2 -> 0; matrix products, arithmetic and copies ran while one was open for 11% -> 0% of each run, Pallas kernels for 0% -> 0%
where the time goes in v1:
time: 62.5 us; the launch traced here: 62.3 us
  Pallas kernels  60.1 us (96%)
  local copies, waits for them, and re-layouts  2.19 us (4%)
    pallas_call x1, Pallas kernels, key_values(): pl.pallas_call(functools.partial(gather_multiply, mp_size), out_shape=jax...  54.3 us
    pallas_call x1, Pallas kernels, place_slots(): pl.pallas_call(functools.partial(place_kernel, 2 * MAXLEN), grid=(half_sl...  5.8 us
    unnamed x8, local copies, waits for them, and re-layouts  2.19 us

profile of v1, /device:TPU:0, one launch (start us, length us, event | category | flops | bytes accessed | tf_op | source)
XLA Modules:
  0.0 62.3 jit_solution(11914727193386015042)
XLA Ops:
  0.0 0.0 copy-start.1
  0.0 0.0 copy-start.2
  0.0 0.0 copy-start.3
  0.0 54.3 %gather_multiply.1 = bf16[8,128,2048]{2,1,0:T(8,128)(2,1)} custom-call(f32[64,4096]{1,0:T(8,128)} %x_ref.1, bf16[2048,2,1024]{2,1,0:T(2,128)(2,1)} %bitcast.3), custom_call_target="tpu_custom_call" | custom-call | tf_op jit(solution)/shard_map/gather_multiply/pallas_call | solution.py:204
  54.3 0.0 copy-done.1
  54.3 0.0 copy-done.2
  54.3 0.0 copy-done.3
  54.3 0.0 copy-start
  54.3 2.2 %copy-done = bf16[8,128,2048]{2,1,0:T(8,128)(2,1)S(1)} copy-done((bf16[8,128,2048]{2,1,0:T(8,128)(2,1)S(1)}, bf16[8,128,2048]{2,1,0:T(8,128)(2,1)}, u32[]{:S(2)}) %copy-start) | copy-done | bytes 4194328
  56.5 5.8 %place_slots.1 = bf16[1,8,128,2,1024]{4,3,2,1,0:T(2,128)(2,1)} custom-call(s32[16]{0:T(128)S(1)} %copy-done.1, s32[16]{0:T(128)S(1)} %copy-done.2, s32[16]{0:T(128)S(1)} %copy-done.3, bf16[1024,2048]{1,0:T(8,128)(2,1)S(1)} %bitcast.2), custom_call_target="tpu_custom_call" | custom-call | tf_op jit(solution)/shard_map/place_slots/pallas_call | solution.py:265
Async XLA Ops:
  0.0 54.3 %copy-start.1 = (s32[16]{0:T(128)S(1)}, s32[16]{0:T(128)}, u32[]{:S(2)}) copy-start(s32[16]{0:T(128)} %lengths.1) | copy-start | bytes 196
  0.0 54.3 %copy-start.2 = (s32[16]{0:T(128)S(1)}, s32[16]{0:T(128)}, u32[]{:S(2)}) copy-start(s32[16]{0:T(128)} %slot_of.1) | copy-start | bytes 196
  0.0 54.3 %copy-start.3 = (s32[16]{0:T(128)S(1)}, s32[16]{0:T(128)}, u32[]{:S(2)}) copy-start(s32[16]{0:T(128)} %order.1) | copy-start | bytes 196
  54.3 2.2 %copy-start = (bf16[8,128,2048]{2,1,0:T(8,128)(2,1)S(1)}, bf16[8,128,2048]{2,1,0:T(8,128)(2,1)}, u32[]{:S(2)}) copy-start(bf16[8,128,2048]{2,1,0:T(8,128)(2,1)} %gather_multiply.1) | copy-start | bytes 12582916

commit v2 on v1

--- a/solution.py
+++ b/solution.py
@@ -37,8 +37,8 @@
     return jnp.where(inside[:, None], taken, jnp.zeros((), values.dtype))
 
 
-def gather_multiply(mp_size, x_ref, w_hbm, kv_ref, w_raw, w_flat, x_send, rows, acc, part, other, *sems):
-    w_sem, x_ss, x_rs, r_ss, r_rs, l_ss, l_rs, p_ss, p_rs = sems
+def gather_multiply(mp_size, x_ref, w_hbm, kv_hbm, w_raw, w_flat, x_send, rows, acc, part, other, done, *sems):
+    w_sem, x_ss, x_rs, r_ss, r_rs, l_ss, l_rs, p_ss, p_rs, o_sem = sems
     mesh_id = pl.DeviceIdType.MESH
     ring = 2 * mp_size
     count, half = x_send.shape
@@ -116,37 +116,52 @@
             start = pl.multiple_of(i * depth + t * piece, piece)
             w_flat[pl.ds(start, piece), :] = w_raw[pl.ds(start, piece)].reshape(piece, width)
 
-    def swap_part(m, at):
+    def swap_part(m, at, side):
         return pltpu.make_async_remote_copy(
-            src_ref=part.at[at], dst_ref=other.at[at], send_sem=p_ss.at[m], recv_sem=p_rs.at[m],
+            src_ref=part.at[at, side], dst_ref=other.at[at, side],
+            send_sem=p_ss.at[m, side], recv_sem=p_rs.at[m, side],
             device_id=partner, device_id_type=mesh_id,
         )
 
+    def store(m, at, side):
+        rows_at = pl.ds(pl.multiple_of(at * 2 * count, 2 * count), 2 * count)
+        return pltpu.make_async_copy(
+            done.at[at, side], kv_hbm.at[side, rows_at, :], o_sem.at[m, side]
+        )
+
+    side_width = width // 2
+    columns = 256 if side_width % 256 == 0 else 128
+
     def multiply(chips, m):
-        columns = 256
-
-        @pl.loop(0, width // columns)
-        def _(t):
-            span = pl.ds(pl.multiple_of(t * columns, columns), columns)
-            left = jnp.concatenate([rows[c].reshape(2 * count, half) for c in chips], axis=0)
-            product = jnp.dot(left, w_flat[:, span], preferred_element_type=jnp.float32)
+        for side in range(2):
+
+            @pl.loop(0, side_width // columns)
+            def _(t):
+                start = pl.multiple_of(t * columns, columns)
+                span = pl.ds(start, columns)
+                wide = pl.ds(pl.multiple_of(side * side_width + start, columns), columns)
+                left = jnp.concatenate([rows[c].reshape(2 * count, half) for c in chips], axis=0)
+                product = jnp.dot(left, w_flat[:, wide], preferred_element_type=jnp.float32)
+                for i, c in enumerate(chips):
+                    one = product[i * 2 * count : (i + 1) * 2 * count]
+                    acc[c, side, :, span] = one
+                    part[c, side, :, span] = one.astype(jnp.bfloat16)
+
             for i, c in enumerate(chips):
-                one = product[i * 2 * count : (i + 1) * 2 * count]
-                acc[c, :, span] = one
-                part[c, :, span] = one.astype(jnp.bfloat16)
-
-        for i, c in enumerate(chips):
-            swap_part(m + i, c).start()
+                swap_part(m + i, c, side).start()
 
     def finish(chips, m):
-        for i, c in enumerate(chips):
-            swap_part(m + i, c).wait_recv()
-
-            @pl.loop(0, 2 * count // 16)
-            def _(t):
-                span = pl.ds(pl.multiple_of(t * 16, 16), 16)
-                total = acc[c, span, :] + other[c, span, :].astype(jnp.float32)
-                kv_ref[c, span, :] = total.astype(jnp.bfloat16)
+        for side in range(2):
+            for i, c in enumerate(chips):
+                swap_part(m + i, c, side).wait_recv()
+
+                @pl.loop(0, 2 * count // 32)
+                def _(t):
+                    span = pl.ds(pl.multiple_of(t * 32, 32), 32)
+                    total = acc[c, side, span, :] + other[c, side, span, :].astype(jnp.float32)
+                    done[c, side, span, :] = total.astype(jnp.bfloat16)
+
+                store(m + i, c, side).start()
 
     send(0, 1).start()
     send(0, -1).start()
@@ -161,14 +176,13 @@
     for k in range(ring - 1):
         if k == ring - 2:
             finish(*waiting)
+        ahead = k + 2
         arrived(k, 1)
+        if ahead <= ring - 2:
+            send(ahead, 1).start()
         arrived(k, -1)
-        ahead = k + 2
         if ahead < ring - 2:
-            send(ahead, 1).start()
             send(ahead, -1).start()
-        elif ahead == ring - 2:
-            send(ahead, 1).start()
         elif ahead == ring - 1:
             send(ring - 2, -1).start()
         if k == 0:
@@ -179,20 +193,25 @@
         elif k % 2 == 1:
             d = (k + 1) // 2
             chips = [chip(-d), chip(d)]
+            if d == 1:
+                finish(*waiting)
             multiply(chips, 2 * d - 1)
+            waiting = (chips, 2 * d - 1)
+        elif k < ring - 2:
             finish(*waiting)
-            waiting = (chips, 2 * d - 1)
     multiply([chip(reach)], ring - 1)
     finish([chip(reach)], ring - 1)
     swap_rows().wait_send()
     for k in range(ring - 1):
         send(k, 1).wait_send()
         send(k, -1).wait_send()
-    swap_part(0, mine).wait_send()
+    blocks = [mine]
     for d in range(1, reach):
-        swap_part(2 * d - 1, chip(-d)).wait_send()
-        swap_part(2 * d, chip(d)).wait_send()
-    swap_part(ring - 1, chip(reach)).wait_send()
+        blocks += [chip(-d), chip(d)]
+    for m, c in enumerate(blocks + [chip(reach)]):
+        for side in range(2):
+            swap_part(m, c, side).wait_send()
+            store(m, c, side).wait()
 
 
 def key_values(enc_rows, weight, mp_size):
@@ -200,18 +219,19 @@
     half, _, head_width = weight.shape
     width, ring = 2 * head_width, 2 * mp_size
     dma = pltpu.SemaphoreType.DMA
-    block = (ring, 2 * count, width)
-    packed = pl.pallas_call(
+    block = (ring, 2, 2 * count, head_width)
+    return pl.pallas_call(
         functools.partial(gather_multiply, mp_size),
-        out_shape=jax.ShapeDtypeStruct(block, jnp.bfloat16),
+        out_shape=jax.ShapeDtypeStruct((2, ring * 2 * count, head_width), jnp.bfloat16),
         in_specs=[pl.BlockSpec(memory_space=pltpu.VMEM), pl.BlockSpec(memory_space=pl.ANY)],
-        out_specs=pl.BlockSpec(memory_space=pltpu.VMEM),
+        out_specs=pl.BlockSpec(memory_space=pl.ANY),
         scratch_shapes=[
             pltpu.VMEM(weight.shape, jnp.bfloat16),
             pltpu.VMEM((half, width), jnp.bfloat16),
             pltpu.VMEM((count, half), jnp.bfloat16),
             pltpu.VMEM((ring, 2, count, half), jnp.bfloat16),
             pltpu.VMEM(block, jnp.float32),
+            pltpu.VMEM(block, jnp.bfloat16),
             pltpu.VMEM(block, jnp.bfloat16),
             pltpu.VMEM(block, jnp.bfloat16),
             dma((4,)),
@@ -221,20 +241,34 @@
             dma((ring - 1,)),
             dma((ring - 1,)),
             dma((ring - 1,)),
-            dma((ring,)),
-            dma((ring,)),
+            dma((ring, 2)),
+            dma((ring, 2)),
+            dma((ring, 2)),
         ],
         compiler_params=pltpu.CompilerParams(
             collective_id=0, has_side_effects=True, vmem_limit_bytes=56 << 20
         ),
         name="gather_multiply",
     )(enc_rows, weight)
-    return packed.reshape(ring * 2 * count, width)
-
-
-def place_kernel(window, lengths, slot_of, order, kv_ref, out_ref, begins, request):
+
+
+def place_kernel(lengths, slot_of, order, kv_hbm, out_ref, windows, begins, request, sems):
     slot_count = lengths.shape[0]
-    step = pl.program_id(0)
+    step, steps = pl.program_id(0), pl.num_programs(0)
+    window = windows.shape[2]
+    first = lax.axis_index("pool") * steps
+
+    def lookup(s):
+        who = request[first + s]
+        begin = begins[who]
+        base = jnp.minimum((begin // 16) * 16, kv_hbm.shape[1] - window)
+        return lengths[who], begin, pl.multiple_of(base, 16)
+
+    def fetch(s):
+        base = lookup(s)[2]
+        return pltpu.make_async_copy(
+            kv_hbm.at[:, pl.ds(base, window), :], windows.at[s], sems.at[s]
+        )
 
     @pl.when(step == 0)
     def _():
@@ -245,32 +279,40 @@
 
         lax.fori_loop(0, slot_count, one, jnp.int32(0))
 
-    who = request[lax.axis_index("pool") * pl.num_programs(0) + step]
-    size, begin = lengths[who], begins[who]
-    base = pl.multiple_of(jnp.minimum((begin // 16) * 16, kv_ref.shape[0] - window), 16)
+        @pl.loop(0, steps)
+        def _(s):
+            fetch(s).start()
+
+    size, begin, base = lookup(step)
     shape = (MAXLEN, window)
     position = lax.broadcasted_iota(jnp.int32, shape, 0)
     source = lax.broadcasted_iota(jnp.int32, shape, 1)
     chosen = (source == position + (begin - base)) & (position < size)
     picked = jnp.where(chosen, 1.0, 0.0).astype(jnp.bfloat16)
-    taken = jnp.dot(picked, kv_ref[pl.ds(base, window), :], preferred_element_type=jnp.float32)
-    out_ref[0, 0] = taken.astype(jnp.bfloat16).reshape(out_ref.shape[2:])
+    fetch(step).wait()
+    taken = [
+        jnp.dot(picked, windows[step, c], preferred_element_type=jnp.float32).astype(jnp.bfloat16)
+        for c in range(2)
+    ]
+    out_ref[0, 0] = jnp.concatenate(taken, axis=1).reshape(out_ref.shape[2:])
 
 
 def place_slots(key_value, lengths, slot_of, order, half_slots):
-    width = key_value.shape[1]
+    head_width = key_value.shape[2]
     slot_count = lengths.shape[0]
     smem = pl.BlockSpec(memory_space=pltpu.SMEM)
-    shape = (1, half_slots, MAXLEN, 2, width // 2)
+    shape = (1, half_slots, MAXLEN, 2, head_width)
     return pl.pallas_call(
-        functools.partial(place_kernel, 2 * MAXLEN),
+        place_kernel,
         grid=(half_slots,),
         out_shape=jax.ShapeDtypeStruct(shape, jnp.bfloat16),
-        in_specs=[smem, smem, smem, pl.BlockSpec(memory_space=pltpu.VMEM)],
-        out_specs=pl.BlockSpec((1, 1, MAXLEN, 2, width // 2), lambda s: (0, s, 0, 0, 0)),
+        in_specs=[smem, smem, smem, pl.BlockSpec(memory_space=pl.ANY)],
+        out_specs=pl.BlockSpec((1, 1, MAXLEN, 2, head_width), lambda s: (0, s, 0, 0, 0)),
         scratch_shapes=[
+            pltpu.VMEM((half_slots, 2, MAXLEN + 16, head_width), jnp.bfloat16),
             pltpu.SMEM((slot_count,), jnp.int32),
             pltpu.SMEM((slot_count,), jnp.int32),
+            pltpu.SemaphoreType.DMA((half_slots,)),
         ],
         compiler_params=pltpu.CompilerParams(vmem_limit_bytes=32 << 20),
         name="place_slots",

time: 62.5 us -> 61.3 us (0.981)
  Pallas kernels: 60.1 us -> 58.6 us
    pallas_call x1, Pallas kernels: 54.3 us -> 52 us  [key_values(): pl.pallas_call(functools.partial(gather_multiply, mp_size), out_shape=jax...]
    pallas_call x1, Pallas kernels: 5.8 us -> 6.63 us  [place_slots(): pl.pallas_call(place_kernel, grid=(half_slots,), out_shape=jax.ShapeDtype...]
where the time goes in v2:
time: 61.3 us; the launch traced here: 60.9 us
  Pallas kernels  58.6 us (96%)
  local copies, waits for them, and re-layouts  2.19 us (4%)
    pallas_call x1, Pallas kernels, key_values(): pl.pallas_call(functools.partial(gather_multiply, mp_size), out_shape=jax...  52 us
    pallas_call x1, Pallas kernels, place_slots(): pl.pallas_call(place_kernel, grid=(half_slots,), out_shape=jax.ShapeDtype...  6.63 us
    unnamed x8, local copies, waits for them, and re-layouts  2.19 us

profile of v2, /device:TPU:0, one launch (start us, length us, event | category | flops | bytes accessed | tf_op | source)
XLA Modules:
  0.0 60.9 jit_solution(6378335072134905187)
XLA Ops:
  0.0 0.0 copy-start.1
  0.0 0.0 copy-start.2
  0.0 0.0 copy-start.3
  0.0 52.0 %gather_multiply.1.kv_hbm = bf16[2,1024,1024]{2,1,0:T(8,128)(2,1)} custom-call(f32[64,4096]{1,0:T(8,128)} %x_ref.1, bf16[2048,2,1024]{2,1,0:T(2,128)(2,1)} %bitcast.1), custom_call_target="tpu_custom_call" | custom-call | tf_op jit(solution)/shard_map/gather_multiply/pallas_call | solution.py:223
  52.0 0.0 copy-done.1
  52.0 0.0 copy-done.2
  52.1 0.0 copy-done.3
  52.1 0.0 copy-start
  52.1 2.2 %copy-done = bf16[2,1024,1024]{2,1,0:T(8,128)(2,1)S(1)} copy-done((bf16[2,1024,1024]{2,1,0:T(8,128)(2,1)S(1)}, bf16[2,1024,1024]{2,1,0:T(8,128)(2,1)}, u32[]{:S(2)}) %copy-start) | copy-done | bytes 4194328
  54.3 6.6 %place_slots.1 = bf16[1,8,128,2,1024]{4,3,2,1,0:T(2,128)(2,1)} custom-call(s32[16]{0:T(128)S(1)} %copy-done.1, s32[16]{0:T(128)S(1)} %copy-done.2, s32[16]{0:T(128)S(1)} %copy-done.3, bf16[2,1024,1024]{2,1,0:T(8,128)(2,1)S(1)} %copy-done), custom_call_target="tpu_custom_call" | custom-call | tf_op jit(solution)/shard_map/place_slots/pallas_call | solution.py:305
Async XLA Ops:
  0.0 52.0 %copy-start.1 = (s32[16]{0:T(128)S(1)}, s32[16]{0:T(128)}, u32[]{:S(2)}) copy-start(s32[16]{0:T(128)} %lengths.1) | copy-start | bytes 196
  0.0 52.0 %copy-start.2 = (s32[16]{0:T(128)S(1)}, s32[16]{0:T(128)}, u32[]{:S(2)}) copy-start(s32[16]{0:T(128)} %slot_of.1) | copy-start | bytes 196
  0.0 52.1 %copy-start.3 = (s32[16]{0:T(128)S(1)}, s32[16]{0:T(128)}, u32[]{:S(2)}) copy-start(s32[16]{0:T(128)} %order.1) | copy-start | bytes 196
  52.1 2.2 %copy-start = (bf16[2,1024,1024]{2,1,0:T(8,128)(2,1)S(1)}, bf16[2,1024,1024]{2,1,0:T(8,128)(2,1)}, u32[]{:S(2)}) copy-start(bf16[2,1024,1024]{2,1,0:T(8,128)(2,1)} %gather_multiply.1.kv_hbm) | copy-start | bytes 12582916

commit v3 on v2

--- a/solution.py
+++ b/solution.py
@@ -123,11 +123,9 @@
             device_id=partner, device_id_type=mesh_id,
         )
 
-    def store(m, at, side):
+    def store(m, at):
         rows_at = pl.ds(pl.multiple_of(at * 2 * count, 2 * count), 2 * count)
-        return pltpu.make_async_copy(
-            done.at[at, side], kv_hbm.at[side, rows_at, :], o_sem.at[m, side]
-        )
+        return pltpu.make_async_copy(done.at[at], kv_hbm.at[rows_at], o_sem.at[m])
 
     side_width = width // 2
     columns = 256 if side_width % 256 == 0 else 128
@@ -151,17 +149,21 @@
                 swap_part(m + i, c, side).start()
 
     def finish(chips, m):
-        for side in range(2):
-            for i, c in enumerate(chips):
+        piece = 16
+        for i, c in enumerate(chips):
+            for side in range(2):
                 swap_part(m + i, c, side).wait_recv()
 
-                @pl.loop(0, 2 * count // 32)
-                def _(t):
-                    span = pl.ds(pl.multiple_of(t * 32, 32), 32)
-                    total = acc[c, side, span, :] + other[c, side, span, :].astype(jnp.float32)
-                    done[c, side, span, :] = total.astype(jnp.bfloat16)
-
-                store(m + i, c, side).start()
+            @pl.loop(0, 2 * count // piece)
+            def _(t):
+                span = pl.ds(pl.multiple_of(t * piece, piece), piece)
+                total = [
+                    (acc[c, side, span, :] + other[c, side, span, :].astype(jnp.float32)).astype(jnp.bfloat16)
+                    for side in range(2)
+                ]
+                done[c, span] = jnp.concatenate(total, axis=1).reshape(piece, 2, side_width)
+
+            store(m + i, c).start()
 
     send(0, 1).start()
     send(0, -1).start()
@@ -211,7 +213,7 @@
     for m, c in enumerate(blocks + [chip(reach)]):
         for side in range(2):
             swap_part(m, c, side).wait_send()
-            store(m, c, side).wait()
+        store(m, c).wait()
 
 
 def key_values(enc_rows, weight, mp_size):
@@ -222,7 +224,7 @@
     block = (ring, 2, 2 * count, head_width)
     return pl.pallas_call(
         functools.partial(gather_multiply, mp_size),
-        out_shape=jax.ShapeDtypeStruct((2, ring * 2 * count, head_width), jnp.bfloat16),
+        out_shape=jax.ShapeDtypeStruct((ring * 2 * count, 2, head_width), jnp.bfloat16),
         in_specs=[pl.BlockSpec(memory_space=pltpu.VMEM), pl.BlockSpec(memory_space=pl.ANY)],
         out_specs=pl.BlockSpec(memory_space=pl.ANY),
         scratch_shapes=[
@@ -233,7 +235,7 @@
             pltpu.VMEM(block, jnp.float32),
             pltpu.VMEM(block, jnp.bfloat16),
             pltpu.VMEM(block, jnp.bfloat16),
-            pltpu.VMEM(block, jnp.bfloat16),
+            pltpu.VMEM((ring, 2 * count, 2, head_width), jnp.bfloat16),
             dma((4,)),
             dma,
             dma,
@@ -243,7 +245,7 @@
             dma((ring - 1,)),
             dma((ring, 2)),
             dma((ring, 2)),
-            dma((ring, 2)),
+            dma((ring,)),
         ],
         compiler_params=pltpu.CompilerParams(
             collective_id=0, has_side_effects=True, vmem_limit_bytes=56 << 20
@@ -252,49 +254,49 @@
     )(enc_rows, weight)
 
 
-def place_kernel(lengths, slot_of, order, kv_hbm, out_ref, windows, begins, request, sems):
+def place_kernel(lengths, slot_of, order, kv_hbm, out_hbm, windows, begins, request, in_sems, out_sems):
     slot_count = lengths.shape[0]
-    step, steps = pl.program_id(0), pl.num_programs(0)
-    window = windows.shape[2]
-    first = lax.axis_index("pool") * steps
+    half_slots = windows.shape[0]
+    first = lax.axis_index("pool") * half_slots
+
+    def one(i, begin):
+        begins[order[i]] = begin
+        request[slot_of[i]] = i
+        return begin + lengths[order[i]]
+
+    lax.fori_loop(0, slot_count, one, jnp.int32(0))
 
     def lookup(s):
         who = request[first + s]
-        begin = begins[who]
-        base = jnp.minimum((begin // 16) * 16, kv_hbm.shape[1] - window)
-        return lengths[who], begin, pl.multiple_of(base, 16)
+        base = jnp.minimum(begins[who], kv_hbm.shape[0] - MAXLEN)
+        return lengths[who], base, begins[who] - base
 
     def fetch(s):
-        base = lookup(s)[2]
+        base = lookup(s)[1]
         return pltpu.make_async_copy(
-            kv_hbm.at[:, pl.ds(base, window), :], windows.at[s], sems.at[s]
-        )
-
-    @pl.when(step == 0)
-    def _():
-        def one(i, begin):
-            begins[order[i]] = begin
-            request[slot_of[i]] = i
-            return begin + lengths[order[i]]
-
-        lax.fori_loop(0, slot_count, one, jnp.int32(0))
-
-        @pl.loop(0, steps)
-        def _(s):
-            fetch(s).start()
-
-    size, begin, base = lookup(step)
-    shape = (MAXLEN, window)
-    position = lax.broadcasted_iota(jnp.int32, shape, 0)
-    source = lax.broadcasted_iota(jnp.int32, shape, 1)
-    chosen = (source == position + (begin - base)) & (position < size)
-    picked = jnp.where(chosen, 1.0, 0.0).astype(jnp.bfloat16)
-    fetch(step).wait()
-    taken = [
-        jnp.dot(picked, windows[step, c], preferred_element_type=jnp.float32).astype(jnp.bfloat16)
-        for c in range(2)
-    ]
-    out_ref[0, 0] = jnp.concatenate(taken, axis=1).reshape(out_ref.shape[2:])
+            kv_hbm.at[pl.ds(base, MAXLEN)], windows.at[s, pl.ds(0, MAXLEN)], in_sems.at[s]
+        )
+
+    def write(s):
+        skip = lookup(s)[2]
+        return pltpu.make_async_copy(
+            windows.at[s, pl.ds(skip, MAXLEN)], out_hbm.at[0, s], out_sems.at[s]
+        )
+
+    for s in range(half_slots):
+        fetch(s).start()
+    blank = jnp.zeros(windows.shape[2:], windows.dtype)
+    for s in range(half_slots):
+        size, _, skip = lookup(s)
+        fetch(s).wait()
+
+        @pl.loop(skip + size, skip + MAXLEN)
+        def _(j):
+            windows[s, j] = blank
+
+        write(s).start()
+    for s in range(half_slots):
+        write(s).wait()
 
 
 def place_slots(key_value, lengths, slot_of, order, half_slots):
@@ -304,17 +306,17 @@
     shape = (1, half_slots, MAXLEN, 2, head_width)
     return pl.pallas_call(
         place_kernel,
-        grid=(half_slots,),
         out_shape=jax.ShapeDtypeStruct(shape, jnp.bfloat16),
         in_specs=[smem, smem, smem, pl.BlockSpec(memory_space=pl.ANY)],
-        out_specs=pl.BlockSpec((1, 1, MAXLEN, 2, head_width), lambda s: (0, s, 0, 0, 0)),
+        out_specs=pl.BlockSpec(memory_space=pl.ANY),
         scratch_shapes=[
-            pltpu.VMEM((half_slots, 2, MAXLEN + 16, head_width), jnp.bfloat16),
+            pltpu.VMEM((half_slots, 2 * MAXLEN, 2, head_width), jnp.bfloat16),
             pltpu.SMEM((slot_count,), jnp.int32),
             pltpu.SMEM((slot_count,), jnp.int32),
             pltpu.SemaphoreType.DMA((half_slots,)),
+            pltpu.SemaphoreType.DMA((half_slots,)),
         ],
-        compiler_params=pltpu.CompilerParams(vmem_limit_bytes=32 << 20),
+        compiler_params=pltpu.CompilerParams(vmem_limit_bytes=56 << 20),
         name="place_slots",
     )(lengths, slot_of, order, key_value)
 

time: 61.3 us -> 58.6 us (0.956)
  local copies, waits for them, and re-layouts: 2.19 us -> 0 us
  Pallas kernels: 58.6 us -> 57.9 us
    unnamed x8 -> x0, local copies, waits for them, and re-layouts: 2.19 us -> none
    pallas_call x1, Pallas kernels: 6.63 us -> 5.59 us  [place_slots(): pl.pallas_call(place_kernel, out_shape=jax.ShapeDtypeStruct(shape, jnp.bf...]
where the time goes in v3:
time: 58.6 us; the launch traced here: 57.9 us
  Pallas kernels  57.9 us (99%)
    pallas_call x1, Pallas kernels, key_values(): pl.pallas_call(functools.partial(gather_multiply, mp_size), out_shape=jax...  52.4 us
    pallas_call x1, Pallas kernels, place_slots(): pl.pallas_call(place_kernel, out_shape=jax.ShapeDtypeStruct(shape, jnp.bf...  5.59 us

profile of v3, /device:TPU:0, one launch (start us, length us, event | category | flops | bytes accessed | tf_op | source)
XLA Modules:
  0.0 57.9 jit_solution(9836255923918025576)
XLA Ops:
  0.0 52.4 %gather_multiply.1.kv_hbm = bf16[1024,2,1024]{2,1,0:T(2,128)(2,1)} custom-call(f32[64,4096]{1,0:T(8,128)} %x_ref.1, bf16[2048,2,1024]{2,1,0:T(2,128)(2,1)} %bitcast.1), custom_call_target="tpu_custom_call" | custom-call | tf_op jit(solution)/shard_map/gather_multiply/pallas_call | solution.py:225
  52.4 5.6 %place_slots.1 = bf16[1,8,128,2,1024]{4,3,2,1,0:T(2,128)(2,1)} custom-call(s32[16]{0:T(128)} %lengths.1, s32[16]{0:T(128)} %slot_of.1, s32[16]{0:T(128)} %order.1, bf16[1024,2,1024]{2,1,0:T(2,128)(2,1)} %gather_multiply.1.kv_hbm), custom_call_target="tpu_custom_call" | custom-call | tf_op jit(solution)/shard_map/place_slots/pallas_call | solution.py:307

commit v4 on v3

--- a/solution.py
+++ b/solution.py
@@ -7,6 +7,7 @@
 from jax.experimental.pallas import tpu as pltpu
 from jax.sharding import PartitionSpec as P
 MAXLEN = 128
+BLANK = 16
 
 
 def pack_tables(lengths, slot_of, order):
@@ -76,36 +77,31 @@
         pl.semaphore_signal(barrier, inc=1, device_id=target, device_id_type=mesh_id)
     mine = chip(0)
     rows[mine, pool] = x_ref[:, pl.ds(pl.multiple_of(pool * half, half), half)].astype(jnp.bfloat16)
-    x_send[...] = x_ref[:, pl.ds(pl.multiple_of((1 - pool) * half, half), half)].astype(jnp.bfloat16)
     pl.semaphore_wait(barrier, 3)
 
-    def send(k, direction):
-        last = k == ring - 2
-        second = (k % 2 == 1) or (last and direction < 0)
-        core = 1 - pool if second else pool
-        slot = rows.at[chip(-direction * (k // 2)), core]
+    def ring_copy(k, direction, hops):
+        step = min(k, ring - 2)
+        second = (k % 2 == 1) if k < ring - 2 else direction < 0
+        slot = rows.at[chip(-direction * (step // 2 + hops)), 1 - pool if second else pool]
+        if k >= ring - 2:
+            slot = slot.at[:, pl.ds((k - step) * (half // 2), half // 2)]
         ss, rs = (r_ss, r_rs) if direction > 0 else (l_ss, l_rs)
         return pltpu.make_async_remote_copy(
             src_ref=slot, dst_ref=slot, send_sem=ss.at[k], recv_sem=rs.at[k],
             device_id=device(direction), device_id_type=mesh_id,
         )
 
+    def send(k, direction):
+        return ring_copy(k, direction, 0)
+
+    def arrived(k, direction):
+        ring_copy(k, direction, 1).wait_recv()
+
     def swap_rows():
         return pltpu.make_async_remote_copy(
             src_ref=x_send, dst_ref=rows.at[mine, pool], send_sem=x_ss, recv_sem=x_rs,
             device_id=partner, device_id_type=mesh_id,
         )
-
-    def arrived(k, direction):
-        last = k == ring - 2
-        second = (k % 2 == 1) or (last and direction < 0)
-        core = 1 - pool if second else pool
-        slot = rows.at[chip(-direction * (k // 2 + 1)), core]
-        ss, rs = (r_ss, r_rs) if direction > 0 else (l_ss, l_rs)
-        pltpu.make_async_remote_copy(
-            src_ref=slot, dst_ref=slot, send_sem=ss.at[k], recv_sem=rs.at[k],
-            device_id=device(direction), device_id_type=mesh_id,
-        ).wait_recv()
 
     def flatten(i):
         weight_copy(i).wait()
@@ -130,7 +126,7 @@
     side_width = width // 2
     columns = 256 if side_width % 256 == 0 else 128
 
-    def multiply(chips, m):
+    def multiply(chips, m, begin=0, size=half, is_last=True):
         for side in range(2):
 
             @pl.loop(0, side_width // columns)
@@ -138,15 +134,24 @@
                 start = pl.multiple_of(t * columns, columns)
                 span = pl.ds(start, columns)
                 wide = pl.ds(pl.multiple_of(side * side_width + start, columns), columns)
-                left = jnp.concatenate([rows[c].reshape(2 * count, half) for c in chips], axis=0)
-                product = jnp.dot(left, w_flat[:, wide], preferred_element_type=jnp.float32)
+                left = jnp.concatenate(
+                    [rows[c, :, :, begin : begin + size].reshape(2 * count, size) for c in chips],
+                    axis=0,
+                )
+                product = jnp.dot(
+                    left, w_flat[begin : begin + size, wide], preferred_element_type=jnp.float32
+                )
                 for i, c in enumerate(chips):
                     one = product[i * 2 * count : (i + 1) * 2 * count]
+                    if begin > 0:
+                        one = one + acc[c, side, :, span]
                     acc[c, side, :, span] = one
-                    part[c, side, :, span] = one.astype(jnp.bfloat16)
-
-            for i, c in enumerate(chips):
-                swap_part(m + i, c, side).start()
+                    if is_last:
+                        part[c, side, :, span] = one.astype(jnp.bfloat16)
+
+            if is_last:
+                for i, c in enumerate(chips):
+                    swap_part(m + i, c, side).start()
 
     def finish(chips, m):
         piece = 16
@@ -167,6 +172,7 @@
 
     send(0, 1).start()
     send(0, -1).start()
+    x_send[...] = x_ref[:, pl.ds(pl.multiple_of((1 - pool) * half, half), half)].astype(jnp.bfloat16)
     swap_rows().start()
     swap_rows().wait_recv()
     send(1, 1).start()
@@ -175,18 +181,19 @@
     flatten(1)
     reach = ring // 2
     waiting = None
-    for k in range(ring - 1):
-        if k == ring - 2:
-            finish(*waiting)
+    for k in range(ring - 2):
         ahead = k + 2
         arrived(k, 1)
         if ahead <= ring - 2:
             send(ahead, 1).start()
+        if ahead == ring - 2:
+            send(ring - 1, 1).start()
         arrived(k, -1)
         if ahead < ring - 2:
             send(ahead, -1).start()
         elif ahead == ring - 1:
             send(ring - 2, -1).start()
+            send(ring - 1, -1).start()
         if k == 0:
             flatten(2)
             flatten(3)
@@ -199,12 +206,16 @@
                 finish(*waiting)
             multiply(chips, 2 * d - 1)
             waiting = (chips, 2 * d - 1)
-        elif k < ring - 2:
+        else:
             finish(*waiting)
-    multiply([chip(reach)], ring - 1)
+    finish(*waiting)
+    for part_of in range(2):
+        arrived(ring - 2 + part_of, 1)
+        arrived(ring - 2 + part_of, -1)
+        multiply([chip(reach)], ring - 1, part_of * (half // 2), half // 2, part_of == 1)
     finish([chip(reach)], ring - 1)
     swap_rows().wait_send()
-    for k in range(ring - 1):
+    for k in range(ring):
         send(k, 1).wait_send()
         send(k, -1).wait_send()
     blocks = [mine]
@@ -239,10 +250,10 @@
             dma((4,)),
             dma,
             dma,
-            dma((ring - 1,)),
-            dma((ring - 1,)),
-            dma((ring - 1,)),
-            dma((ring - 1,)),
+            dma((ring,)),
+            dma((ring,)),
+            dma((ring,)),
+            dma((ring,)),
             dma((ring, 2)),
             dma((ring, 2)),
             dma((ring,)),
@@ -285,14 +296,14 @@
 
     for s in range(half_slots):
         fetch(s).start()
-    blank = jnp.zeros(windows.shape[2:], windows.dtype)
+    blank = jnp.zeros((BLANK, *windows.shape[2:]), windows.dtype)
     for s in range(half_slots):
         size, _, skip = lookup(s)
         fetch(s).wait()
 
-        @pl.loop(skip + size, skip + MAXLEN)
+        @pl.loop(0, (MAXLEN - size + BLANK - 1) // BLANK)
         def _(j):
-            windows[s, j] = blank
+            windows[s, pl.ds(skip + size + j * BLANK, BLANK)] = blank
 
         write(s).start()
     for s in range(half_slots):
@@ -310,7 +321,7 @@
         in_specs=[smem, smem, smem, pl.BlockSpec(memory_space=pl.ANY)],
         out_specs=pl.BlockSpec(memory_space=pl.ANY),
         scratch_shapes=[
-            pltpu.VMEM((half_slots, 2 * MAXLEN, 2, head_width), jnp.bfloat16),
+            pltpu.VMEM((half_slots, 2 * MAXLEN + BLANK, 2, head_width), jnp.bfloat16),
             pltpu.SMEM((slot_count,), jnp.int32),
             pltpu.SMEM((slot_count,), jnp.int32),
             pltpu.SemaphoreType.DMA((half_slots,)),
@@ -331,6 +342,7 @@
         and 2 <= mp_size <= 8
         and enc_rows.shape[0] % 16 == 0
         and head_width % 128 == 0
+        and kv_weight.shape[1] % 256 == 0
     )
     if ring_fits:
         key_value = key_values(enc_rows, kv_weight[0], mp_size)

time: 58.6 us -> 58.3 us (level)
    pallas_call x1, Pallas kernels: 52.4 us -> 53.8 us  [key_values(): pl.pallas_call(functools.partial(gather_multiply, mp_size), out_shape=jax...]
    pallas_call x1, Pallas kernels: 5.59 us -> 4.39 us  [place_slots(): pl.pallas_call(place_kernel, out_shape=jax.ShapeDtypeStruct(shape, jnp.bf...]
where the time goes in v4:
time: 58.3 us; the launch traced here: 58.2 us
  Pallas kernels  58.2 us (100%)
    pallas_call x1, Pallas kernels, key_values(): pl.pallas_call(functools.partial(gather_multiply, mp_size), out_shape=jax...  53.8 us
    pallas_call x1, Pallas kernels, place_slots(): pl.pallas_call(place_kernel, out_shape=jax.ShapeDtypeStruct(shape, jnp.bf...  4.39 us

profile of v4, /device:TPU:0, one launch (start us, length us, event | category | flops | bytes accessed | tf_op | source)
XLA Modules:
  0.0 58.2 jit_solution(17746809824557443517)
XLA Ops:
  0.0 53.8 %gather_multiply.1.kv_hbm = bf16[1024,2,1024]{2,1,0:T(2,128)(2,1)} custom-call(f32[64,4096]{1,0:T(8,128)} %x_ref.1, bf16[2048,2,1024]{2,1,0:T(2,128)(2,1)} %bitcast.1), custom_call_target="tpu_custom_call" | custom-call | tf_op jit(solution)/shard_map/gather_multiply/pallas_call | solution.py:236
  53.8 4.4 %place_slots.1 = bf16[1,8,128,2,1024]{4,3,2,1,0:T(2,128)(2,1)} custom-call(s32[16]{0:T(128)} %lengths.1, s32[16]{0:T(128)} %slot_of.1, s32[16]{0:T(128)} %order.1, bf16[1024,2,1024]{2,1,0:T(2,128)(2,1)} %gather_multiply.1.kv_hbm), custom_call_target="tpu_custom_call" | custom-call | tf_op jit(solution)/shard_map/place_slots/pallas_call | solution.py:318
